TPU v7x, 32 devices: a whole 2x2x4 slice. The times are simulated.
32 devices in a mesh: row: 4 (over y, x), col: 4 (over z), chan: 2 (over core).
Axes of the slice: x: 2, y: 2, z: 4, core: 2. Of those that a mesh axis runs over, the one named last changes fastest.
Arguments:
- samples: bfloat16 [8192, 2, 2048], P(('chan', 'col'), None, 'row'), parts along dimension 0, may hold values from -6 to 6
- sky_model: bfloat16 [8192, 2, 4096], P(('chan', 'row'), None, 'col'), parts along dimension 0, may hold values from -128 to 128, as said below
- initial_gains: float32 [2, 8192], P(None, ('chan', 'row', 'col')), parts along dimension 1, may hold values from -3 to 3, as said below
Outputs:
- calibrated: float32 [2, 8192], P(None, ('chan', 'row', 'col')), parts along dimension 1
There are 2 independent parts, one for each index of `chan`. A program takes and returns all parts, laid end to end along the dimension named above; each array names one. Nothing has to cross between parts.
Inputs may be any that keep to these rules, and one draw needn't show every extreme that they name: sky_model is Hermitian: sky_model[q,0,p] = sky_model[p,0,q] and sky_model[q,1,p] = -sky_model[p,1,q]. `initial_gains`: every initial gain has magnitude between 0.3 and 3.
All inputs are finite; a program needn't handle non-finite values.
Results may differ from a plain program's by a relative error of at most 0.0003.
Values may be sent and summed in bfloat16 or wider, within the bound.
A program may use at most 192 MiB of HBM per device.

v0:
```python
import jax
import jax.numpy as jnp
from jax import lax
from jax.sharding import PartitionSpec as P

ITERS = 3


def body(samples, sky_model, initial_gains):
    row_count = lax.axis_size("row")
    column_count = lax.axis_size("col")
    row_index = lax.axis_index("row")
    column_index = lax.axis_index("col")
    block_column = samples.shape[0]
    block_row = sky_model.shape[0]
    share_size = initial_gains.shape[1]
    contract_last = (((1,), (1,)), ((), ()))
    upper_limit = lax.Precision.HIGHEST
    own_start = (row_index * column_count + column_index) * share_size
    flattened = samples.reshape(block_column, -1)
    rotated = jnp.concatenate([-samples[:, 1, :], samples[:, 0, :]], axis=1)
    right_side = jnp.concatenate([flattened, rotated], axis=0)
    all_antennas = lax.all_gather(flattened, "col", axis=0, tiled=True)
    vis_tile = lax.psum_scatter(
        lax.dot_general(
            all_antennas, right_side, contract_last, preferred_element_type=jnp.float32
        ),
        "row",
        scatter_dimension=0,
        tiled=True,
    )
    vis_real = vis_tile[:, :block_column]
    vis_imag = vis_tile[:, block_column:]
    model_real = sky_model[:, 0, :].astype(jnp.float32)
    model_imag = sky_model[:, 1, :].astype(jnp.float32)
    global_rows = row_index * block_row + lax.broadcasted_iota(
        jnp.int32, (block_row, block_column), 0
    )
    global_columns = column_index * block_column + lax.broadcasted_iota(
        jnp.int32, (block_row, block_column), 1
    )
    cross_mask = (global_rows != global_columns).astype(jnp.float32)
    weight_real = (vis_real * model_real + vis_imag * model_imag) * cross_mask
    weight_imag = (vis_real * model_imag - vis_imag * model_real) * cross_mask
    model_power = (model_real * model_real + model_imag * model_imag) * cross_mask
    stacked = jnp.concatenate([weight_real, weight_imag], axis=0)
    row_gains = lax.all_gather(initial_gains, "col", axis=1, tiled=True)
    everything = row_gains
    for iteration in range(ITERS):
        gain_real = row_gains[0]
        gain_imag = row_gains[1]
        left_rows = jnp.stack(
            [jnp.concatenate([gain_real, -gain_imag]), jnp.concatenate([gain_imag, gain_real])]
        )
        totals = jnp.dot(left_rows, stacked, precision=upper_limit)
        energy = jnp.dot(
            gain_real * gain_real + gain_imag * gain_imag, model_power, precision=upper_limit
        )
        totals, energy = (totals, energy)
        totals, energy = (
            lax.psum_scatter(totals, "row", scatter_dimension=1, tiled=True),
            lax.psum_scatter(energy, "row", scatter_dimension=0, tiled=True),
        )
        updated = totals / energy[None, :]
        if iteration == 1:
            previous = lax.dynamic_slice_in_dim(
                everything, (column_index * row_count + row_index) * share_size, share_size, 1
            )
            updated = 0.5 * (updated + previous)
        gain_block = lax.all_gather(updated, "row", axis=1, tiled=True)
        everything = lax.all_gather(gain_block, "col", axis=1, tiled=True)
        row_gains = lax.dynamic_slice_in_dim(everything, row_index * block_row, block_row, 1)
    return lax.dynamic_slice_in_dim(everything, own_start, share_size, 1)


def solution(mesh):
    return jax.shard_map(
        body,
        mesh=mesh,
        in_specs=(
            P(("chan", "col"), None, "row"),
            P(("chan", "row"), None, "col"),
            P(None, ("chan", "row", "col")),
        ),
        out_specs=P(None, ("chan", "row", "col")),
        check_vma=False,
    )
```

profile of v0, /device:TPU:0, one launch (start us, length us, event | category | flops | bytes accessed | tf_op | source)
XLA Modules:
  0.0 657.7 jit_solution(2612143580094805734)
XLA Ops:
  6.5 0.0 copy-start.2
  6.5 0.0 all-gather.2.cloned.1.call-start
  6.5 3.6 copy.25
  10.2 0.0 all-gather.2.cloned.1.call-update
  10.2 0.0 reduce-scatter.11.cloned.1.call-start
  10.3 0.0 copy-done.2
  10.3 3.0 fusion.56
  13.2 0.0 copy-start.3
  13.3 1.2 copy_bitcast_fusion
  14.5 148.2 %all-gather.2.cloned.1.call-done = bf16[4096,1024]{1,0:T(8,128)(2,1)} async-done(((bf16[1024,1024]{1,0:T(8,128)(2,1)}), bf16[4096,1024]{1,0:T(8,128)(2,1)}) %all-gather.2.cloned.1.call-update) | async-done | bytes 8388624 | tf_op jit(solution)/shard_map/all_gather | solution.py:23
  162.7 0.0 copy-done.3
  162.7 23.4 %convolution_bitcast_fusion = f32[4096,2048]{0,1:T(8,128)} fusion(bf16[4096,1024]{1,0:T(8,128)(2,1)} %all-gather.2.cloned.1.call-done, bf16[1024,512]{1,0:T(8,128)(2,1)S(1)} %get-tuple-element.23, bf16[1024,512]{1,0:T(8,128)(2,1)} %get-tuple-element.24, bf16[1024,1024]{1,0:T(8,128)(2,1)S(1)} %bitcast.77), kind=kOutput, calls=%fused_computation | convolution fusion | flops 17192452096 | bytes 46137344 | tf_op jit(solution)/shard_map/dot_general | solution.py:25
  186.1 0.0 reduce-scatter.11.cloned.1.call-update
  186.1 0.0 reduce-scatter.13.cloned.1.call-start
  186.1 9.9 %fusion.55 = (bf16[1024,1,1024]{2,1,0:T(2,128)(2,1)}, bf16[1024,1,1024]{2,1,0:T(2,128)(2,1)}) fusion(bf16[1024,2,1024]{2,1,0:T(2,128)(2,1)} %param.4), kind=kLoop, calls=%fused_computation.76 | loop fusion | bytes 8388608 | tf_op jit(solution)/shard_map/slice | solution.py:35
  196.1 9.1 %copy.23 = bf16[1024,1,1024]{0,2,1:T(8,128)(2,1)S(1)} copy(bf16[1024,1,1024]{2,1,0:T(2,128)(2,1)} %get-tuple-element.8) | data formatting | bytes 4194304
  205.1 0.0 copy-start.4
  205.2 10.7 %copy.24 = bf16[1024,1,1024]{0,2,1:T(8,128)(2,1)} copy(bf16[1024,1,1024]{2,1,0:T(2,128)(2,1)} %get-tuple-element.7) | data formatting | bytes 4194304
  215.8 0.0 copy-done.4
  215.8 12.0 %all_gather.24 = f32[2,1024]{1,0:T(2,128)S(1)} all-gather(f32[2,256]{1,0:T(2,128)S(1)} %copy-done.4), channel_id=1, replica_groups=mesh['row'=4,'col'=4,'chan'=2] {'col'}, dimensions={1}, use_global_device_ids=true | all-gather | bytes 10240 | tf_op jit(solution)/shard_map/all_gather | solution.py:47
  227.9 245.2 %reduce-scatter.11.cloned.1.call-done = f32[1024,2048]{0,1:T(8,128)} async-done(((f32[4096,2048]{0,1:T(8,128)}), f32[1024,2048]{0,1:T(8,128)}) %reduce-scatter.11.cloned.1.call-update) | async-done | bytes 8388624 | tf_op jit(solution)/shard_map/reduce_scatter | solution.py:24
  473.1 5.1 compare_select_fusion.1
  478.3 0.0 copy-start
  478.3 0.0 copy-start.1
  478.3 1.9 copy-done
  480.2 1.2 copy-done.1
  481.5 7.4 %fusion.17 = f32[1024,2]{1,0:T(8,128)} fusion(f32[1024,1024]{0,1:T(8,128)S(1)} %get-tuple-element.6, f32[1024,1024]{0,1:T(8,128)S(1)} %get-tuple-element.5, f32[1,2048]{1,0:T(1,128)S(1)} %bitcast.88, f32[1,2048]{1,0:T(1,128)S(1)} %bitcast.87), kind=kOutput, calls=%fused_computation.25 | convolution fusion | flops 52432896 | bytes 8413184
  488.9 0.0 copy-start.5
  488.9 0.0 reduce-scatter.13.cloned.1.call-update
  488.9 0.0 reduce-scatter.15.cloned.1.call-start
  489.0 5.7 fusion.34
  494.7 0.0 copy-done.5
  494.7 0.6 dynamic-slice
  495.9 9.0 %all-reduce = f32[1024]{0:T(1024)S(1)} all-reduce(f32[1024]{0:T(1024)S(1)} %bitcast.96), channel_id=4, replica_groups=mesh['row'=4,'col'=4,'chan'=2] {'row'}, use_global_device_ids=true, to_apply=%region_2.0.clone | all-reduce | flops 1024 | bytes 8192
  504.9 0.1 dynamic-slice.1
  505.0 9.0 %reduce-scatter.13.cloned.1.call-done = f32[256,2]{1,0:T(8,128)} async-done(((f32[1024,2]{1,0:T(8,128)}), f32[256,2]{1,0:T(8,128)}) %reduce-scatter.13.cloned.1.call-update) | async-done | bytes 2064
  514.0 1.0 copy.16
  515.0 8.2 %all_gather.26 = f32[2,1024]{1,0:T(2,128)S(1)} all-gather(f32[2,256]{1,0:T(2,128)S(1)} %broadcast_divide_fusion.1), channel_id=1, replica_groups=mesh['row'=4,'col'=4,'chan'=2] {'row'}, dimensions={1}, use_global_device_ids=true | all-gather | bytes 10240 | tf_op jit(solution)/shard_map/all_gather | solution.py:70
  523.2 13.1 %all_gather.27 = f32[2,4096]{1,0:T(2,128)S(1)} all-gather(f32[2,1024]{1,0:T(2,128)S(1)} %all_gather.26), channel_id=1, replica_groups=mesh['row'=4,'col'=4,'chan'=2] {'col'}, dimensions={1}, use_global_device_ids=true | all-gather | bytes 40960 | tf_op jit(solution)/shard_map/all_gather | solution.py:71
  536.3 0.1 fusion.58
  536.4 9.8 %fusion.18 = f32[1024,2]{1,0:T(8,128)} fusion(f32[1024,1024]{0,1:T(8,128)} %copy-done.1, f32[1024,1024]{0,1:T(8,128)} %copy-done, f32[1,2048]{1,0:T(1,128)S(1)} %bitcast.92, f32[1,2048]{1,0:T(1,128)S(1)} %bitcast.91), kind=kOutput, calls=%fused_computation.26 | convolution fusion | flops 52432896 | bytes 8413184
  546.2 0.0 reduce-scatter.15.cloned.1.call-update
  546.2 0.0 reduce-scatter.17.cloned.1.call-start
  546.3 5.7 fusion.32
  552.0 8.9 %all-reduce.1 = f32[1024]{0:T(1024)S(1)} all-reduce(f32[1024]{0:T(1024)S(1)} %bitcast.98), channel_id=6, replica_groups=mesh['row'=4,'col'=4,'chan'=2] {'row'}, use_global_device_ids=true, to_apply=%region_4.0.clone | all-reduce | flops 1024 | bytes 8192
  560.9 0.1 dynamic-slice.3
  561.0 10.3 %reduce-scatter.15.cloned.1.call-done = f32[256,2]{1,0:T(8,128)} async-done(((f32[1024,2]{1,0:T(8,128)}), f32[256,2]{1,0:T(8,128)}) %reduce-scatter.15.cloned.1.call-update) | async-done | bytes 2064
  571.2 1.0 copy.18
  572.2 8.0 %all_gather.28 = f32[2,1024]{1,0:T(2,128)S(1)} all-gather(f32[2,256]{1,0:T(2,128)S(1)} %fusion.45), channel_id=1, replica_groups=mesh['row'=4,'col'=4,'chan'=2] {'row'}, dimensions={1}, use_global_device_ids=true | all-gather | bytes 10240 | tf_op jit(solution)/shard_map/all_gather | solution.py:70
  580.2 13.4 %all_gather.29 = f32[2,4096]{1,0:T(2,128)S(1)} all-gather(f32[2,1024]{1,0:T(2,128)S(1)} %all_gather.28), channel_id=1, replica_groups=mesh['row'=4,'col'=4,'chan'=2] {'col'}, dimensions={1}, use_global_device_ids=true | all-gather | bytes 40960 | tf_op jit(solution)/shard_map/all_gather | solution.py:71
  593.6 0.1 fusion.57
  593.7 9.8 %fusion.19 = f32[1024,2]{1,0:T(8,128)} fusion(f32[1024,1024]{0,1:T(8,128)} %copy-done.1, f32[1024,1024]{0,1:T(8,128)} %copy-done, f32[1,2048]{1,0:T(1,128)S(1)} %bitcast.90, f32[1,2048]{1,0:T(1,128)S(1)} %bitcast.89), kind=kOutput, calls=%fused_computation.27 | convolution fusion | flops 52432896 | bytes 8413184
  603.5 0.0 reduce-scatter.17.cloned.1.call-update
  603.5 5.7 fusion.30
  609.2 9.0 %all-reduce.2 = f32[1024]{0:T(1024)S(1)} all-reduce(f32[1024]{0:T(1024)S(1)} %bitcast.97), channel_id=8, replica_groups=mesh['row'=4,'col'=4,'chan'=2] {'row'}, use_global_device_ids=true, to_apply=%region_6.0.clone | all-reduce | flops 1024 | bytes 8192
  618.1 0.1 dynamic-slice.5
  618.2 10.3 %reduce-scatter.17.cloned.1.call-done = f32[256,2]{1,0:T(8,128)} async-done(((f32[1024,2]{1,0:T(8,128)}), f32[256,2]{1,0:T(8,128)}) %reduce-scatter.17.cloned.1.call-update) | async-done | bytes 2064
  628.5 1.0 copy.20
  629.5 8.0 %all_gather.30 = f32[2,1024]{1,0:T(2,128)S(1)} all-gather(f32[2,256]{1,0:T(2,128)S(1)} %broadcast_divide_fusion), channel_id=1, replica_groups=mesh['row'=4,'col'=4,'chan'=2] {'row'}, dimensions={1}, use_global_device_ids=true | all-gather | bytes 10240 | tf_op jit(solution)/shard_map/all_gather | solution.py:70
  637.5 13.1 %all_gather.31 = f32[2,4096]{1,0:T(2,128)S(1)} all-gather(f32[2,1024]{1,0:T(2,128)S(1)} %all_gather.30), channel_id=1, replica_groups=mesh['row'=4,'col'=4,'chan'=2] {'col'}, dimensions={1}, use_global_device_ids=true | all-gather | bytes 40960 | tf_op jit(solution)/shard_map/all_gather | solution.py:71
  650.6 0.6 constant_dynamic-slice_fusion.1
  (11 shorter events, 0.1 us)
Async XLA Ops:
  6.5 3.7 copy-start.2
  6.5 156.2 %all-gather.2.cloned.1.call-start = ((), (), s32[]{:S(2)}) async-start(), calls=%async_computation.4 | async-start | bytes 10485760 | tf_op jit(solution)/shard_map/all_gather | solution.py:23
  10.2 462.9 %reduce-scatter.11.cloned.1.call-start = ((), (), s32[]{:S(2)}) async-start(), calls=%async_computation.5 | async-start | bytes 41943040 | tf_op jit(solution)/shard_map/reduce_scatter | solution.py:24
  13.2 149.4 %copy-start.3 = (bf16[128,8,2,512]{3,1,2,0:T(8,128)(2,1)S(1)}, bf16[128,8,2,512]{3,1,2,0:T(8,128)(2,1)}, u32[]{:S(2)}) copy-start(bf16[128,8,2,512]{3,1,2,0:T(8,128)(2,1)} %copy.25) | copy-start | bytes 6291460
  186.1 327.9 %reduce-scatter.13.cloned.1.call-start = ((), (), s32[]{:S(2)}) async-start(), calls=%async_computation.6 | async-start | bytes 655360
  205.1 10.7 %copy-start.4 = (f32[2,256]{1,0:T(2,128)S(1)}, f32[2,256]{1,0:T(2,128)}, u32[]{:S(2)}) copy-start(f32[2,256]{1,0:T(2,128)} %param.5) | copy-start | bytes 6148
  478.3 2.0 copy-start
  478.3 3.2 copy-start.1
  488.9 5.8 copy-start.5
  488.9 82.3 %reduce-scatter.15.cloned.1.call-start = ((), (), s32[]{:S(2)}) async-start(), calls=%async_computation.7 | async-start | bytes 655360
  546.2 82.3 %reduce-scatter.17.cloned.1.call-start = ((), (), s32[]{:S(2)}) async-start(), calls=%async_computation.8 | async-start | bytes 655360
Sparse Core Ops, SparseCore 0:
  10.3 152.3 all-gather.1
  186.2 286.8 reduce-scatter.10
  489.0 24.8 reduce-scatter.12
  546.3 24.8 reduce-scatter.14
  603.6 24.8 reduce-scatter.16
where the time goes:
time: 659 us; the launch traced here: 658 us
  waiting for transfers between devices  423 us (64%)
  blocking collectives  103 us (16%)
  matrix products  67.4 us (10%)
  local copies, waits for them, and re-layouts  44 us (7%)
  between operations  13.9 us (2%)
    reduce_scatter x1, waiting for transfers between devices, body(): lax.psum_scatter(lax.dot_general(all_antennas, right_side, contract_last,...  245 us
    all_gather x1, waiting for transfers between devices, body(): all_antennas = lax.all_gather(flattened, 'col', axis=0, tiled=True)  148 us
    all_gather x3, blocking collectives, body(): everything = lax.all_gather(gain_block, 'col', axis=1, tiled=True)  39.7 us
    unnamed x22, local copies, waits for them, and re-layouts  30.4 us
    unnamed x8, waiting for transfers between devices  29.6 us
    unnamed x3, matrix products  26.9 us
    unnamed x3, blocking collectives  26.9 us
    all_gather x3, blocking collectives, body(): gain_block = lax.all_gather(updated, 'row', axis=1, tiled=True)  24.2 us
  transfers between devices with their start and end apart: 5, of which 5 were waited for; matrix products, arithmetic and copies ran while one was open for 8% of the time, Pallas kernels for 0%

commit v1 on v0

--- a/solution.py
+++ b/solution.py
@@ -1,9 +1,343 @@
+import functools
+
 import jax
 import jax.numpy as jnp
 from jax import lax
+from jax.experimental import pallas as pl
+from jax.experimental.pallas import tpu as pltpu
 from jax.sharding import PartitionSpec as P
 
 ITERS = 3
+MESH = pl.DeviceIdType.MESH
+CONTRACT_LAST = (((1,), (1,)), ((), ()))
+
+
+def remote(src, dst, send, recv, row, col):
+    return pltpu.make_async_remote_copy(
+        src_ref=src,
+        dst_ref=dst,
+        send_sem=send,
+        recv_sem=recv,
+        device_id={"row": row, "col": col},
+        device_id_type=MESH,
+    )
+
+
+def landed(ref, sem):
+    pltpu.make_async_copy(ref, ref, sem).wait()
+
+
+def calibrate(
+    n, own, model, gains, out, chain, left, right, vr, vi, power, qr, qi, tr, ti, gp0, gq0,
+    abuf, bbuf, ain, bin_, gin,
+    up_send, fwd_send, chain_recv, left_send, left_recv, right_send, right_recv, local_sem,
+    gp_send, gp_recv, gq_send, gq_recv, a_send, a_recv, b_send, b_recv, g_send, g_recv,
+):
+    r = lax.axis_index("row")
+    c = lax.axis_index("col")
+    block = own.shape[1]
+    half = own.shape[2] // 2
+    share = gains.shape[1]
+    diag = r == c
+    off = r != c
+
+    barrier = pltpu.get_barrier_semaphore()
+    for step in range(1, n * n):
+        other = lax.rem(r * n + c + step, n * n)
+        pl.semaphore_signal(
+            barrier, inc=1, device_id={"row": other // n, "col": lax.rem(other, n)}, device_id_type=MESH
+        )
+    pl.semaphore_wait(barrier, n * n - 1)
+
+    up = remote(own.at[0], chain.at[c], up_send.at[0], chain_recv.at[c], r, c + 1)
+    down = remote(own.at[1], chain.at[c], up_send.at[1], chain_recv.at[c], r, c - 1)
+    pl.when(c < n - 1)(up.start)
+    pl.when(c > 0)(down.start)
+
+    def right_copy(k):
+        h = jnp.where(k < c, 0, 1)
+        return remote(own.at[h], right.at[r], right_send.at[k], right_recv.at[r], k, c)
+
+    def left_copy(k):
+        return remote(chain.at[k], left.at[r], left_send.at[k], left_recv.at[r], k, c)
+
+    def own_left_copy():
+        return remote(own.at[0], left.at[r], left_send.at[c], left_recv.at[r], c, c)
+
+    for step in range(1, n):
+        right_copy(lax.rem(r + step, n)).start()
+    pl.when(off)(lambda: own_left_copy().start())
+
+    def gq_copy(j):
+        return remote(gains, gq0.at[c], gq_send.at[j], gq_recv.at[c], r, j)
+
+    def gp_copy(i):
+        return remote(gains, gp0.at[c], gp_send.at[i], gp_recv.at[c], i, r)
+
+    for k in range(n):
+        pl.when(k != c)(lambda k=k: gq_copy(k).start())
+        pl.when(jnp.logical_or(k != r, off))(lambda k=k: gp_copy(k).start())
+    gq0[c] = gains[...]
+
+    @pl.when(diag)
+    def _():
+        gp0[c] = gains[...]
+
+    rows_step = 32
+    lane = lax.broadcasted_iota(jnp.int32, (rows_step, block), 1) + c * block
+    sub = lax.broadcasted_iota(jnp.int32, (rows_step, block), 0) + r * block
+
+    @pl.loop(0, block // rows_step)
+    def _(s):
+        rows = pl.ds(pl.multiple_of(s * rows_step, rows_step), rows_step)
+        mr = model[0, rows, :].astype(jnp.float32)
+        mi = model[1, rows, :].astype(jnp.float32)
+        keep = sub + s * rows_step != lane
+        power[rows, :] = jnp.where(keep, mr * mr + mi * mi, 0.0)
+        vr[rows, :] = jnp.zeros((rows_step, block), jnp.float32)
+        vi[rows, :] = jnp.zeros((rows_step, block), jnp.float32)
+
+    def local_left(src, sem):
+        copy = pltpu.make_async_copy(src, left.at[r], sem)
+        copy.start()
+        copy.wait()
+
+    def arrived(k, onward):
+        landed(chain.at[k], chain_recv.at[k])
+        copy = remote(chain.at[k], chain.at[k], fwd_send.at[k], chain_recv.at[k], r, c + onward)
+        pl.when(jnp.logical_and(c + onward >= 0, c + onward < n))(copy.start)
+        pl.when(k != r)(lambda: left_copy(k).start())
+        pl.when(k == r)(lambda: local_left(chain.at[k], local_sem.at[0]))
+
+    for step in range(1, n):
+        pl.when(c >= step)(lambda: arrived(c - step, 1))
+        pl.when(c + step < n)(lambda: arrived(c + step, -1))
+    pl.when(diag)(lambda: local_left(own.at[0], local_sem.at[0]))
+    mine = pltpu.make_async_copy(own.at[jnp.where(r < c, 0, 1)], right.at[r], local_sem.at[1])
+    mine.start()
+    mine.wait()
+
+    tile = min(256, block)
+
+    def multiply(a_ref, b_ref, k):
+        @pl.loop(0, block // tile)
+        def _(s):
+            rows = pl.ds(pl.multiple_of(s * tile, tile), tile)
+            a = a_ref[k, rows, :]
+            b = b_ref[k]
+            dot = functools.partial(
+                lax.dot_general, dimension_numbers=CONTRACT_LAST, preferred_element_type=jnp.float32
+            )
+            vr[rows, :] += dot(a, b)
+            vi[rows, :] += dot(a[:, half:], b[:, :half]) - dot(a[:, :half], b[:, half:])
+
+    @pl.loop(0, n)
+    def _(step):
+        k = lax.rem(r + step, n)
+
+        @pl.when(step > 0)
+        def _():
+            landed(left.at[k], left_recv.at[k])
+            landed(right.at[k], right_recv.at[k])
+
+        pl.when(off)(lambda: multiply(left, right, k))
+
+        @pl.when(diag)
+        def _():
+            multiply(left, left, k)
+            multiply(right, right, k)
+
+    @pl.loop(0, block // rows_step)
+    def _(s):
+        rows = pl.ds(pl.multiple_of(s * rows_step, rows_step), rows_step)
+        mr = model[0, rows, :].astype(jnp.float32)
+        mi = model[1, rows, :].astype(jnp.float32)
+        keep = sub + s * rows_step != lane
+        a, b = vr[rows, :], vi[rows, :]
+        vr[rows, :] = jnp.where(keep, a * mr + b * mi, 0.0)
+        vi[rows, :] = jnp.where(keep, a * mi - b * mr, 0.0)
+
+    for k in range(n):
+        pl.when(k != c)(lambda k=k: landed(gq0.at[k], gq_recv.at[k]))
+        pl.when(jnp.logical_or(k != c, off))(lambda k=k: landed(gp0.at[k], gp_recv.at[k]))
+
+    def start_gains(ref):
+        return [jnp.concatenate([ref[k, part : part + 1, :] for k in range(n)], axis=1) for part in range(2)]
+
+    gp = start_gains(gp0)
+    gq = start_gains(gq0)
+    lanes = 128
+    tiles = block // lanes
+
+    for it in range(ITERS):
+        gpr = jnp.broadcast_to(gp[0], (8, block))
+        gpi = jnp.broadcast_to(gp[1], (8, block))
+        qr[...] = jnp.broadcast_to(gq[0], (lanes, block)).T
+        qi[...] = jnp.broadcast_to(gq[1], (lanes, block)).T
+
+        def fold(x):
+            total = x[:, :lanes]
+            for t in range(1, tiles):
+                total = total + x[:, t * lanes : (t + 1) * lanes]
+            return total
+
+        def sums(s, carry):
+            sum_r, sum_i, sum_e = carry
+            rows = pl.ds(pl.multiple_of(s * 8, 8), 8)
+            wr, wi = vr[rows, :], vi[rows, :]
+            ar, ai = qr[rows, :], qi[rows, :]
+            norm = ar * ar + ai * ai
+            wide = lambda x: jnp.concatenate([x] * tiles, axis=1)
+            ar, ai, norm = wide(ar), wide(ai), wide(norm)
+            tr[rows, :] = fold(wr * gpr + wi * gpi)
+            ti[rows, :] = fold(wr * gpi - wi * gpr)
+            return (
+                sum_r + (wr * ar - wi * ai),
+                sum_i + (wr * ai + wi * ar),
+                sum_e + power[rows, :] * norm,
+            )
+
+        zero = jnp.zeros((8, block), jnp.float32)
+        sum_r, sum_i, sum_e = lax.fori_loop(0, block // 8, sums, (zero, zero, zero))
+        for part, value in enumerate((sum_r, sum_i, sum_e)):
+            abuf[it, part : part + 1, :] = jnp.sum(value, axis=0, keepdims=True)
+        for part, ref in enumerate((tr, ti)):
+            bbuf[it, part : part + 1, :] = jnp.sum(ref[...].T, axis=0, keepdims=True)
+
+        a_copy = remote(abuf.at[it], ain.at[it, r], a_send.at[it], a_recv.at[it, r], c, c)
+        b_copy = remote(bbuf.at[it], bin_.at[it, c], b_send.at[it], b_recv.at[it, c], r, r)
+
+        @pl.when(off)
+        def _():
+            a_copy.start()
+            b_copy.start()
+
+        def p_copy(i):
+            return remote(gin.at[it, 0], gin.at[it, 0], g_send.at[it, 0, i], g_recv.at[it, 0], i, c)
+
+        def q_copy(j):
+            return remote(gin.at[it, 0], gin.at[it, 1], g_send.at[it, 1, j], g_recv.at[it, 1], r, j)
+
+        @pl.when(diag)
+        def _():
+            total = abuf[it]
+            for k in range(n):
+                @pl.when(k != r)
+                def _():
+                    landed(ain.at[it, k], a_recv.at[it, k])
+                    landed(bin_.at[it, k], b_recv.at[it, k])
+
+            ain[it, r] = jnp.zeros_like(total)
+            bin_[it, r] = jnp.zeros_like(total)
+            for k in range(n):
+                total = total + ain[it, k]
+            extra = bin_[it, 0]
+            for k in range(1, n):
+                extra = extra + bin_[it, k]
+            for part in range(2):
+                fresh = (total[part : part + 1] + extra[part : part + 1]) / total[2:3]
+                if it == 1:
+                    fresh = 0.5 * (fresh + gin[0, 0, part : part + 1, :])
+                gin[it, 0, part : part + 1, :] = fresh
+                gin[it, 1, part : part + 1, :] = fresh
+            for k in range(n):
+                @pl.when(k != r)
+                def _():
+                    q_copy(k).start()
+                    if it < ITERS - 1:
+                        p_copy(k).start()
+
+        @pl.when(off)
+        def _():
+            landed(gin.at[it, 1], g_recv.at[it, 1])
+            if it < ITERS - 1:
+                landed(gin.at[it, 0], g_recv.at[it, 0])
+
+        gp = [gin[it, 0, part : part + 1, :] for part in range(2)]
+        gq = [gin[it, 1, part : part + 1, :] for part in range(2)]
+
+    out[...] = gin[ITERS - 1, 1, 0:2, pl.ds(pl.multiple_of(c * share, share), share)]
+
+    pl.when(c < n - 1)(up.wait_send)
+    pl.when(c > 0)(down.wait_send)
+    for step in range(1, n):
+        right_copy(lax.rem(r + step, n)).wait_send()
+    pl.when(off)(lambda: own_left_copy().wait_send())
+
+    def gone(k, onward):
+        copy = remote(chain.at[k], chain.at[k], fwd_send.at[k], chain_recv.at[k], r, c + onward)
+        pl.when(jnp.logical_and(c + onward >= 0, c + onward < n))(copy.wait_send)
+        pl.when(k != r)(lambda: left_copy(k).wait_send())
+
+    for step in range(1, n):
+        pl.when(c >= step)(lambda: gone(c - step, 1))
+        pl.when(c + step < n)(lambda: gone(c + step, -1))
+    for k in range(n):
+        pl.when(k != c)(lambda k=k: gq_copy(k).wait_send())
+        pl.when(jnp.logical_or(k != r, off))(lambda k=k: gp_copy(k).wait_send())
+    for it in range(ITERS):
+        a_copy = remote(abuf.at[it], ain.at[it, r], a_send.at[it], a_recv.at[it, r], c, c)
+        b_copy = remote(bbuf.at[it], bin_.at[it, c], b_send.at[it], b_recv.at[it, c], r, r)
+
+        @pl.when(off)
+        def _():
+            a_copy.wait_send()
+            b_copy.wait_send()
+
+        for k in range(n):
+            @pl.when(jnp.logical_and(diag, k != r))
+            def _():
+                remote(gin.at[it, 0], gin.at[it, 1], g_send.at[it, 1, k], g_recv.at[it, 1], r, k).wait_send()
+                if it < ITERS - 1:
+                    remote(gin.at[it, 0], gin.at[it, 0], g_send.at[it, 0, k], g_recv.at[it, 0], k, c).wait_send()
+
+
+def square_body(n, samples, sky_model, initial_gains):
+    block, _, times = samples.shape
+    half = times // 2
+    halves = samples.reshape(block, 2, 2, half).transpose(2, 0, 1, 3).reshape(2, block, 2 * half)
+    model = sky_model.transpose(1, 0, 2)
+    share = initial_gains.shape[1]
+    dma = pltpu.SemaphoreType.DMA
+    vmem = pltpu.VMEM
+    f32, bf16 = jnp.float32, jnp.bfloat16
+    piece = (n, block, 2 * half)
+    return pl.pallas_call(
+        functools.partial(calibrate, n),
+        out_shape=jax.ShapeDtypeStruct((2, share), f32),
+        in_specs=[pl.BlockSpec(memory_space=pltpu.VMEM)] * 3,
+        out_specs=pl.BlockSpec(memory_space=pltpu.VMEM),
+        scratch_shapes=[
+            vmem(piece, bf16),
+            vmem(piece, bf16),
+            vmem(piece, bf16),
+            vmem((block, block), f32),
+            vmem((block, block), f32),
+            vmem((block, block), f32),
+            vmem((block, 128), f32),
+            vmem((block, 128), f32),
+            vmem((block, 128), f32),
+            vmem((block, 128), f32),
+            vmem((n, 2, share), f32),
+            vmem((n, 2, share), f32),
+            vmem((ITERS, 8, block), f32),
+            vmem((ITERS, 8, block), f32),
+            vmem((ITERS, n, 8, block), f32),
+            vmem((ITERS, n, 8, block), f32),
+            vmem((ITERS, 2, 8, block), f32),
+            dma((2,)), dma((n,)), dma((n,)),
+            dma((n,)), dma((n,)), dma((n,)), dma((n,)), dma((2,)),
+            dma((n,)), dma((n,)), dma((n,)), dma((n,)),
+            dma((ITERS,)), dma((ITERS, n)), dma((ITERS,)), dma((ITERS, n)),
+            dma((ITERS, 2, n)), dma((ITERS, 2)),
+        ],
+        compiler_params=pltpu.CompilerParams(
+            collective_id=0, has_side_effects=True, vmem_limit_bytes=56 * 1024 * 1024
+        ),
+        cost_estimate=pl.CostEstimate(
+            flops=8 * block * block * times * n // 2, bytes_accessed=8 * block * block, transcendentals=0
+        ),
+    )(halves, model, initial_gains)
 
 
 def body(samples, sky_model, initial_gains):
@@ -74,8 +408,10 @@
 
 
 def solution(mesh):
+    n = mesh.shape["row"]
+    square = n == mesh.shape["col"]
     return jax.shard_map(
-        body,
+        functools.partial(square_body, n) if square else body,
         mesh=mesh,
         in_specs=(
             P(("chan", "col"), None, "row"),

time: 659 us -> 184 us (0.28)
  waiting for transfers between devices: 423 us -> 0 us
  Pallas kernels: 0 us -> 171 us
  blocking collectives: 103 us -> 0 us
  matrix products: 67.4 us -> 0 us
  local copies, waits for them, and re-layouts: 44 us -> 12.4 us
  between operations: 13.9 us -> 0.01 us
    reduce_scatter x1 -> x0, waiting for transfers between devices: 245 us -> none  [body(): lax.psum_scatter(lax.dot_general(all_antennas, right_side, contract_last,...]
    pallas_call x0 -> x1, Pallas kernels: none -> 171 us  [square_body(): pl.pallas_call(functools.partial(calibrate, n), out_shape=jax.ShapeDtypeS...]
    all_gather x1 -> x0, waiting for transfers between devices: 148 us -> none  [body(): all_antennas = lax.all_gather(flattened, 'col', axis=0, tiled=True)]
    all_gather x7 -> x0, blocking collectives: 75.9 us -> none  [the longest x3 39.7 us: body(): everything = lax.all_gather(gain_block, 'col', axis=1, tiled=True)]
    dot_general x4 -> x0, matrix products: 40.4 us -> none  [the longest x1 23.4 us: body(): lax.dot_general(all_antennas, right_side, contract_last, preferred_elemen...]
    unnamed x8 -> x0, waiting for transfers between devices: 29.6 us -> none
    unnamed x3 -> x0, matrix products: 26.9 us -> none
    unnamed x3 -> x0, blocking collectives: 26.9 us -> none
  transfers between devices with their start and end apart: 5 -> 0, of which waited for: 5 -> 0; matrix products, arithmetic and copies ran while one was open for 8% -> 0% of each run, Pallas kernels for 0% -> 0%
where the time goes in v1:
time: 184 us; the launch traced here: 183 us
  Pallas kernels  171 us (93%)
  local copies, waits for them, and re-layouts  12.4 us (7%)
    pallas_call x1, Pallas kernels, square_body(): pl.pallas_call(functools.partial(calibrate, n), out_shape=jax.ShapeDtypeS...  171 us
    unnamed x2, local copies, waits for them, and re-layouts  6.68 us
    reshape x2, local copies, waits for them, and re-layouts, square_body(): samples.reshape(block, 2, 2, half).transpose(2, 0, 1, 3)  5.68 us

profile of v1, /device:TPU:0, one launch (start us, length us, event | category | flops | bytes accessed | tf_op | source)
XLA Modules:
  0.0 183.3 jit_solution(15721618542419140225)
XLA Ops:
  0.0 3.0 %copy.10 = bf16[1024,1,2,2,256]{4,3,1,0,2:T(2,128)(2,1)S(1)} copy(bf16[1024,1,2,2,256]{4,3,2,1,0:T(2,128)(2,1)} %bitcast.12) | data formatting | bytes 4194304 | tf_op jit(solution)/shard_map/reshape | solution.py:298
  3.0 2.7 %reshape.7.own = bf16[2,1024,512]{2,1,0:T(8,128)(2,1)} reshape(bf16[2,1024,2,256]{3,2,1,0:T(2,128)(2,1)S(1)} %bitcast.10) | data formatting | bytes 4194304 | tf_op jit(solution)/shard_map/reshape | solution.py:298
  5.7 5.4 %copy.9 = bf16[1024,2,1024]{2,0,1:T(8,128)(2,1)} copy(bf16[1024,2,1024]{2,1,0:T(2,128)(2,1)} %param.4) | data formatting | bytes 8388608 | tf_op args[1]
  11.1 170.9 %shard_map.37 = f32[2,256]{1,0:T(2,128)} custom-call(bf16[2,1024,512]{2,1,0:T(8,128)(2,1)} %reshape.7.own, bf16[2,1024,1024]{2,1,0:T(8,128)(2,1)} %bitcast.11, f32[2,256]{1,0:T(2,128)} %gains.1), custom_call_target="tpu_custom_call" | custom-call | flops 8589934592 | bytes 8388608 | tf_op jit(solution)/shard_map/pallas_call | solution.py:305
  182.0 1.3 copy.12

commit v2 on v1

--- a/solution.py
+++ b/solution.py
@@ -28,7 +28,7 @@
 
 
 def calibrate(
-    n, own, model, gains, out, chain, left, right, vr, vi, power, qr, qi, tr, ti, gp0, gq0,
+    n, own, sky, gains, out, chain, left, right, vr, vi, power, model, qr, qi, tr, ti, gp0, gq0,
     abuf, bbuf, ain, bin_, gin,
     up_send, fwd_send, chain_recv, left_send, left_recv, right_send, right_recv, local_sem,
     gp_send, gp_recv, gq_send, gq_recv, a_send, a_recv, b_send, b_recv, g_send, g_recv,
@@ -38,6 +38,10 @@
     block = own.shape[1]
     half = own.shape[2] // 2
     share = gains.shape[1]
+
+    def mine_at(h):
+        return own.at[:, :, pl.ds(pl.multiple_of(h * half, half), half)]
+
     diag = r == c
     off = r != c
 
@@ -49,20 +53,20 @@
         )
     pl.semaphore_wait(barrier, n * n - 1)
 
-    up = remote(own.at[0], chain.at[c], up_send.at[0], chain_recv.at[c], r, c + 1)
-    down = remote(own.at[1], chain.at[c], up_send.at[1], chain_recv.at[c], r, c - 1)
+    up = remote(mine_at(0), chain.at[c], up_send.at[0], chain_recv.at[c], r, c + 1)
+    down = remote(mine_at(1), chain.at[c], up_send.at[1], chain_recv.at[c], r, c - 1)
     pl.when(c < n - 1)(up.start)
     pl.when(c > 0)(down.start)
 
     def right_copy(k):
         h = jnp.where(k < c, 0, 1)
-        return remote(own.at[h], right.at[r], right_send.at[k], right_recv.at[r], k, c)
+        return remote(mine_at(h), right.at[r], right_send.at[k], right_recv.at[r], k, c)
 
     def left_copy(k):
         return remote(chain.at[k], left.at[r], left_send.at[k], left_recv.at[r], k, c)
 
     def own_left_copy():
-        return remote(own.at[0], left.at[r], left_send.at[c], left_recv.at[r], c, c)
+        return remote(mine_at(0), left.at[r], left_send.at[c], left_recv.at[r], c, c)
 
     for step in range(1, n):
         right_copy(lax.rem(r + step, n)).start()
@@ -90,10 +94,14 @@
     @pl.loop(0, block // rows_step)
     def _(s):
         rows = pl.ds(pl.multiple_of(s * rows_step, rows_step), rows_step)
-        mr = model[0, rows, :].astype(jnp.float32)
-        mi = model[1, rows, :].astype(jnp.float32)
+        pair = sky[rows].astype(jnp.float32)
+        mr, mi = pair[:, 0, :], pair[:, 1, :]
         keep = sub + s * rows_step != lane
-        power[rows, :] = jnp.where(keep, mr * mr + mi * mi, 0.0)
+        mr = jnp.where(keep, mr, 0.0)
+        mi = jnp.where(keep, mi, 0.0)
+        model[0, rows, :] = mr
+        model[1, rows, :] = mi
+        power[rows, :] = mr * mr + mi * mi
         vr[rows, :] = jnp.zeros((rows_step, block), jnp.float32)
         vi[rows, :] = jnp.zeros((rows_step, block), jnp.float32)
 
@@ -112,8 +120,8 @@
     for step in range(1, n):
         pl.when(c >= step)(lambda: arrived(c - step, 1))
         pl.when(c + step < n)(lambda: arrived(c + step, -1))
-    pl.when(diag)(lambda: local_left(own.at[0], local_sem.at[0]))
-    mine = pltpu.make_async_copy(own.at[jnp.where(r < c, 0, 1)], right.at[r], local_sem.at[1])
+    pl.when(diag)(lambda: local_left(mine_at(0), local_sem.at[0]))
+    mine = pltpu.make_async_copy(mine_at(jnp.where(r < c, 0, 1)), right.at[r], local_sem.at[1])
     mine.start()
     mine.wait()
 
@@ -123,13 +131,14 @@
         @pl.loop(0, block // tile)
         def _(s):
             rows = pl.ds(pl.multiple_of(s * tile, tile), tile)
-            a = a_ref[k, rows, :]
-            b = b_ref[k]
+            ar, ai = a_ref[k, 0, rows, :], a_ref[k, 1, rows, :]
+            br, bi = b_ref[k, 0], b_ref[k, 1]
             dot = functools.partial(
                 lax.dot_general, dimension_numbers=CONTRACT_LAST, preferred_element_type=jnp.float32
             )
-            vr[rows, :] += dot(a, b)
-            vi[rows, :] += dot(a[:, half:], b[:, :half]) - dot(a[:, :half], b[:, half:])
+            both = lambda x, y: jnp.concatenate([x, y], axis=1)
+            vr[rows, :] += dot(both(ar, ai), both(br, bi))
+            vi[rows, :] += dot(both(ai, -ar), both(br, bi))
 
     @pl.loop(0, n)
     def _(step):
@@ -150,12 +159,10 @@
     @pl.loop(0, block // rows_step)
     def _(s):
         rows = pl.ds(pl.multiple_of(s * rows_step, rows_step), rows_step)
-        mr = model[0, rows, :].astype(jnp.float32)
-        mi = model[1, rows, :].astype(jnp.float32)
-        keep = sub + s * rows_step != lane
+        mr, mi = model[0, rows, :], model[1, rows, :]
         a, b = vr[rows, :], vi[rows, :]
-        vr[rows, :] = jnp.where(keep, a * mr + b * mi, 0.0)
-        vi[rows, :] = jnp.where(keep, a * mi - b * mr, 0.0)
+        vr[rows, :] = a * mr + b * mi
+        vi[rows, :] = a * mi - b * mr
 
     for k in range(n):
         pl.when(k != c)(lambda k=k: landed(gq0.at[k], gq_recv.at[k]))
@@ -228,7 +235,7 @@
                     landed(bin_.at[it, k], b_recv.at[it, k])
 
             ain[it, r] = jnp.zeros_like(total)
-            bin_[it, r] = jnp.zeros_like(total)
+            bin_[it, r] = jnp.zeros((2, block), jnp.float32)
             for k in range(n):
                 total = total + ain[it, k]
             extra = bin_[it, 0]
@@ -295,13 +302,12 @@
 def square_body(n, samples, sky_model, initial_gains):
     block, _, times = samples.shape
     half = times // 2
-    halves = samples.reshape(block, 2, 2, half).transpose(2, 0, 1, 3).reshape(2, block, 2 * half)
-    model = sky_model.transpose(1, 0, 2)
+    parts = samples.transpose(1, 0, 2)
     share = initial_gains.shape[1]
     dma = pltpu.SemaphoreType.DMA
     vmem = pltpu.VMEM
     f32, bf16 = jnp.float32, jnp.bfloat16
-    piece = (n, block, 2 * half)
+    piece = (n, 2, block, half)
     return pl.pallas_call(
         functools.partial(calibrate, n),
         out_shape=jax.ShapeDtypeStruct((2, share), f32),
@@ -314,17 +320,18 @@
             vmem((block, block), f32),
             vmem((block, block), f32),
             vmem((block, block), f32),
+            vmem((2, block, block), f32),
             vmem((block, 128), f32),
             vmem((block, 128), f32),
             vmem((block, 128), f32),
             vmem((block, 128), f32),
             vmem((n, 2, share), f32),
             vmem((n, 2, share), f32),
-            vmem((ITERS, 8, block), f32),
-            vmem((ITERS, 8, block), f32),
-            vmem((ITERS, n, 8, block), f32),
-            vmem((ITERS, n, 8, block), f32),
-            vmem((ITERS, 2, 8, block), f32),
+            vmem((ITERS, 4, block), f32),
+            vmem((ITERS, 2, block), f32),
+            vmem((ITERS, n, 4, block), f32),
+            vmem((ITERS, n, 2, block), f32),
+            vmem((ITERS, 2, 2, block), f32),
             dma((2,)), dma((n,)), dma((n,)),
             dma((n,)), dma((n,)), dma((n,)), dma((n,)), dma((2,)),
             dma((n,)), dma((n,)), dma((n,)), dma((n,)),
@@ -337,7 +344,7 @@
         cost_estimate=pl.CostEstimate(
             flops=8 * block * block * times * n // 2, bytes_accessed=8 * block * block, transcendentals=0
         ),
-    )(halves, model, initial_gains)
+    )(parts, sky_model, initial_gains)
 
 
 def body(samples, sky_model, initial_gains):

time: 184 us -> 172 us (0.935)
  local copies, waits for them, and re-layouts: 12.4 us -> 4.54 us
  Pallas kernels: 171 us -> 167 us
    reshape x2 -> x0, local copies, waits for them, and re-layouts: 5.68 us -> none  [square_body(): samples.reshape(block, 2, 2, half).transpose(2, 0, 1, 3)]
    pallas_call x1, Pallas kernels: 171 us -> 167 us  [square_body(): pl.pallas_call(functools.partial(calibrate, n), out_shape=jax.ShapeDtypeS...]
    unnamed x2, local copies, waits for them, and re-layouts: 6.68 us -> 4.54 us
where the time goes in v2:
time: 172 us; the launch traced here: 171 us
  Pallas kernels  167 us (97%)
  local copies, waits for them, and re-layouts  4.54 us (3%)
    pallas_call x1, Pallas kernels, square_body(): pl.pallas_call(functools.partial(calibrate, n), out_shape=jax.ShapeDtypeS...  167 us
    unnamed x2, local copies, waits for them, and re-layouts  4.54 us

profile of v2, /device:TPU:0, one launch (start us, length us, event | category | flops | bytes accessed | tf_op | source)
XLA Modules:
  0.0 171.4 jit_solution(11940291064846896211)
XLA Ops:
  0.0 3.3 %copy.6 = bf16[1024,2,512]{2,0,1:T(8,128)(2,1)} copy(bf16[1024,2,512]{2,1,0:T(2,128)(2,1)} %param.3) | data formatting | bytes 4194304 | tf_op args[0]
  3.3 166.9 %shard_map.37 = f32[2,256]{1,0:T(2,128)} custom-call(bf16[2,1024,512]{2,1,0:T(8,128)(2,1)} %bitcast.3, bf16[1024,2,1024]{2,1,0:T(2,128)(2,1)} %sky.1, f32[2,256]{1,0:T(2,128)} %gains.1), custom_call_target="tpu_custom_call" | custom-call | flops 8589934592 | bytes 8388608 | tf_op jit(solution)/shard_map/pallas_call | solution.py:311
  170.2 1.3 copy.8

commit v3 on v2

--- a/solution.py
+++ b/solution.py
@@ -8,6 +8,7 @@
 from jax.sharding import PartitionSpec as P
 
 ITERS = 3
+CHUNKS = 4
 MESH = pl.DeviceIdType.MESH
 CONTRACT_LAST = (((1,), (1,)), ((), ()))
 
@@ -39,8 +40,17 @@
     half = own.shape[2] // 2
     share = gains.shape[1]
 
+    tile = max(block // CHUNKS, 16)
+    chunks = range(block // tile)
+
     def mine_at(h):
         return own.at[:, :, pl.ds(pl.multiple_of(h * half, half), half)]
+
+    def part_of(ref, k, s):
+        return ref.at[k, :, pl.ds(s * tile, tile), :]
+
+    def mine_part(h, s):
+        return own.at[:, pl.ds(s * tile, tile), pl.ds(h * half, half)]
 
     diag = r == c
     off = r != c
@@ -53,24 +63,34 @@
         )
     pl.semaphore_wait(barrier, n * n - 1)
 
-    up = remote(mine_at(0), chain.at[c], up_send.at[0], chain_recv.at[c], r, c + 1)
-    down = remote(mine_at(1), chain.at[c], up_send.at[1], chain_recv.at[c], r, c - 1)
-    pl.when(c < n - 1)(up.start)
-    pl.when(c > 0)(down.start)
+    def up(s):
+        return remote(mine_part(0, s), part_of(chain, c, s), up_send.at[0, s], chain_recv.at[c, s], r, c + 1)
+
+    def down(s):
+        return remote(mine_part(1, s), part_of(chain, c, s), up_send.at[1, s], chain_recv.at[c, s], r, c - 1)
+
+    for s in chunks:
+        pl.when(c < n - 1)(lambda: up(s).start())
+        pl.when(c > 0)(lambda: down(s).start())
 
     def right_copy(k):
         h = jnp.where(k < c, 0, 1)
         return remote(mine_at(h), right.at[r], right_send.at[k], right_recv.at[r], k, c)
 
-    def left_copy(k):
-        return remote(chain.at[k], left.at[r], left_send.at[k], left_recv.at[r], k, c)
-
-    def own_left_copy():
-        return remote(mine_at(0), left.at[r], left_send.at[c], left_recv.at[r], c, c)
+    def left_copy(k, s):
+        return remote(
+            part_of(chain, k, s), part_of(left, r, s), left_send.at[k, s], left_recv.at[r, s], k, c
+        )
+
+    def own_left_copy(s):
+        return remote(
+            mine_part(0, s), part_of(left, r, s), left_send.at[c, s], left_recv.at[r, s], c, c
+        )
 
     for step in range(1, n):
         right_copy(lax.rem(r + step, n)).start()
-    pl.when(off)(lambda: own_left_copy().start())
+    for s in chunks:
+        pl.when(off)(lambda: own_left_copy(s).start())
 
     def gq_copy(j):
         return remote(gains, gq0.at[c], gq_send.at[j], gq_recv.at[c], r, j)
@@ -105,56 +125,75 @@
         vr[rows, :] = jnp.zeros((rows_step, block), jnp.float32)
         vi[rows, :] = jnp.zeros((rows_step, block), jnp.float32)
 
-    def local_left(src, sem):
-        copy = pltpu.make_async_copy(src, left.at[r], sem)
-        copy.start()
-        copy.wait()
-
-    def arrived(k, onward):
-        landed(chain.at[k], chain_recv.at[k])
-        copy = remote(chain.at[k], chain.at[k], fwd_send.at[k], chain_recv.at[k], r, c + onward)
-        pl.when(jnp.logical_and(c + onward >= 0, c + onward < n))(copy.start)
-        pl.when(k != r)(lambda: left_copy(k).start())
-        pl.when(k == r)(lambda: local_left(chain.at[k], local_sem.at[0]))
-
-    for step in range(1, n):
-        pl.when(c >= step)(lambda: arrived(c - step, 1))
-        pl.when(c + step < n)(lambda: arrived(c + step, -1))
-    pl.when(diag)(lambda: local_left(mine_at(0), local_sem.at[0]))
     mine = pltpu.make_async_copy(mine_at(jnp.where(r < c, 0, 1)), right.at[r], local_sem.at[1])
     mine.start()
     mine.wait()
 
-    tile = min(256, block)
-
-    def multiply(a_ref, b_ref, k):
-        @pl.loop(0, block // tile)
+    def multiply(a_ref, b_ref, k, s):
+        rows = pl.ds(pl.multiple_of(s * tile, tile), tile)
+        ar, ai = a_ref[k, 0, rows, :], a_ref[k, 1, rows, :]
+        br, bi = b_ref[k, 0], b_ref[k, 1]
+        dot = functools.partial(
+            lax.dot_general, dimension_numbers=CONTRACT_LAST, preferred_element_type=jnp.float32
+        )
+        both = lambda x, y: jnp.concatenate([x, y], axis=1)
+        vr[rows, :] += dot(both(ar, ai), both(br, bi))
+        vi[rows, :] += dot(both(ai, -ar), both(br, bi))
+
+    @pl.when(diag)
+    def _():
+        copy = pltpu.make_async_copy(mine_at(0), left.at[r], local_sem.at[0])
+        copy.start()
+        copy.wait()
+
+        @pl.loop(0, len(chunks))
         def _(s):
+            multiply(left, left, r, s)
+            multiply(right, right, r, s)
+
+    def onward_copy(k, s, onward):
+        return remote(
+            part_of(chain, k, s), part_of(chain, k, s), fwd_send.at[k, s], chain_recv.at[k, s], r, c + onward
+        )
+
+    def arrived(k, s, onward):
+        landed(part_of(chain, k, s), chain_recv.at[k, s])
+        pl.when(jnp.logical_and(c + onward >= 0, c + onward < n))(lambda: onward_copy(k, s, onward).start())
+        pl.when(k != r)(lambda: left_copy(k, s).start())
+
+    for step in range(1, n):
+        for s in chunks:
+            pl.when(c >= step)(lambda: arrived(c - step, s, 1))
+            pl.when(c + step < n)(lambda: arrived(c + step, s, -1))
+
+    @pl.when(off)
+    def _():
+        @pl.loop(0, len(chunks))
+        def _(s):
+            multiply(chain, right, r, s)
+
+    for step in range(1, n):
+        landed(right.at[lax.rem(r + step, n)], right_recv.at[lax.rem(r + step, n)])
+
+    @pl.loop(0, len(chunks))
+    def _(s):
+        @pl.loop(1, n)
+        def _(step):
+            k = lax.rem(r + step, n)
             rows = pl.ds(pl.multiple_of(s * tile, tile), tile)
-            ar, ai = a_ref[k, 0, rows, :], a_ref[k, 1, rows, :]
-            br, bi = b_ref[k, 0], b_ref[k, 1]
-            dot = functools.partial(
-                lax.dot_general, dimension_numbers=CONTRACT_LAST, preferred_element_type=jnp.float32
-            )
-            both = lambda x, y: jnp.concatenate([x, y], axis=1)
-            vr[rows, :] += dot(both(ar, ai), both(br, bi))
-            vi[rows, :] += dot(both(ai, -ar), both(br, bi))
-
-    @pl.loop(0, n)
-    def _(step):
-        k = lax.rem(r + step, n)
-
-        @pl.when(step > 0)
-        def _():
-            landed(left.at[k], left_recv.at[k])
-            landed(right.at[k], right_recv.at[k])
-
-        pl.when(off)(lambda: multiply(left, right, k))
-
-        @pl.when(diag)
-        def _():
-            multiply(left, left, k)
-            multiply(right, right, k)
+            landed(left.at[k, :, rows, :], left_recv.at[k, s])
+            pl.when(off)(lambda: multiply(left, right, k, s))
+
+    @pl.when(diag)
+    def _():
+        @pl.loop(1, n)
+        def _(step):
+            k = lax.rem(r + step, n)
+
+            @pl.loop(0, len(chunks))
+            def _(s):
+                multiply(left, left, k, s)
+                multiply(right, right, k, s)
 
     @pl.loop(0, block // rows_step)
     def _(s):
@@ -265,20 +304,20 @@
 
     out[...] = gin[ITERS - 1, 1, 0:2, pl.ds(pl.multiple_of(c * share, share), share)]
 
-    pl.when(c < n - 1)(up.wait_send)
-    pl.when(c > 0)(down.wait_send)
     for step in range(1, n):
         right_copy(lax.rem(r + step, n)).wait_send()
-    pl.when(off)(lambda: own_left_copy().wait_send())
-
-    def gone(k, onward):
-        copy = remote(chain.at[k], chain.at[k], fwd_send.at[k], chain_recv.at[k], r, c + onward)
-        pl.when(jnp.logical_and(c + onward >= 0, c + onward < n))(copy.wait_send)
-        pl.when(k != r)(lambda: left_copy(k).wait_send())
-
-    for step in range(1, n):
-        pl.when(c >= step)(lambda: gone(c - step, 1))
-        pl.when(c + step < n)(lambda: gone(c + step, -1))
+
+    def gone(k, s, onward):
+        pl.when(jnp.logical_and(c + onward >= 0, c + onward < n))(lambda: onward_copy(k, s, onward).wait_send())
+        pl.when(k != r)(lambda: left_copy(k, s).wait_send())
+
+    for s in chunks:
+        pl.when(c < n - 1)(lambda: up(s).wait_send())
+        pl.when(c > 0)(lambda: down(s).wait_send())
+        pl.when(off)(lambda: own_left_copy(s).wait_send())
+        for step in range(1, n):
+            pl.when(c >= step)(lambda: gone(c - step, s, 1))
+            pl.when(c + step < n)(lambda: gone(c + step, s, -1))
     for k in range(n):
         pl.when(k != c)(lambda k=k: gq_copy(k).wait_send())
         pl.when(jnp.logical_or(k != r, off))(lambda k=k: gp_copy(k).wait_send())
@@ -332,8 +371,8 @@
             vmem((ITERS, n, 4, block), f32),
             vmem((ITERS, n, 2, block), f32),
             vmem((ITERS, 2, 2, block), f32),
-            dma((2,)), dma((n,)), dma((n,)),
-            dma((n,)), dma((n,)), dma((n,)), dma((n,)), dma((2,)),
+            dma((2, CHUNKS)), dma((n, CHUNKS)), dma((n, CHUNKS)),
+            dma((n, CHUNKS)), dma((n, CHUNKS)), dma((n,)), dma((n,)), dma((2,)),
             dma((n,)), dma((n,)), dma((n,)), dma((n,)),
             dma((ITERS,)), dma((ITERS, n)), dma((ITERS,)), dma((ITERS, n)),
             dma((ITERS, 2, n)), dma((ITERS, 2)),

time: 172 us -> 155 us (0.901)
  Pallas kernels: 167 us -> 151 us
    pallas_call x1, Pallas kernels: 167 us -> 151 us  [square_body(): pl.pallas_call(functools.partial(calibrate, n), out_shape=jax.ShapeDtypeS...]
where the time goes in v3:
time: 155 us
  Pallas kernels  151 us (97%)
  local copies, waits for them, and re-layouts  4.54 us (3%)
    pallas_call x1, Pallas kernels, square_body(): pl.pallas_call(functools.partial(calibrate, n), out_shape=jax.ShapeDtypeS...  151 us
    unnamed x2, local copies, waits for them, and re-layouts  4.54 us

profile of v3, /device:TPU:0, one launch (start us, length us, event | category | flops | bytes accessed | tf_op | source)
XLA Modules:
  0.0 155.1 jit_solution(13406182921095498910)
XLA Ops:
  0.0 3.3 %copy.6 = bf16[1024,2,512]{2,0,1:T(8,128)(2,1)} copy(bf16[1024,2,512]{2,1,0:T(2,128)(2,1)} %param.3) | data formatting | bytes 4194304 | tf_op args[0]
  3.3 150.6 %shard_map.37 = f32[2,256]{1,0:T(2,128)} custom-call(bf16[2,1024,512]{2,1,0:T(8,128)(2,1)} %bitcast.3, bf16[1024,2,1024]{2,1,0:T(2,128)(2,1)} %sky.1, f32[2,256]{1,0:T(2,128)} %gains.1), custom_call_target="tpu_custom_call" | custom-call | flops 8589934592 | bytes 8388608 | tf_op jit(solution)/shard_map/pallas_call | solution.py:350
  153.9 1.3 copy.8

commit v4 on v3

--- a/solution.py
+++ b/solution.py
@@ -69,9 +69,11 @@
     def down(s):
         return remote(mine_part(1, s), part_of(chain, c, s), up_send.at[1, s], chain_recv.at[c, s], r, c - 1)
 
+    ahead = 2
     for s in chunks:
-        pl.when(c < n - 1)(lambda: up(s).start())
-        pl.when(c > 0)(lambda: down(s).start())
+        first = s < ahead
+        pl.when(c < n - 1 if first else c == 0)(lambda: up(s).start())
+        pl.when(c > 0 if first else c == n - 1)(lambda: down(s).start())
 
     def right_copy(k):
         h = jnp.where(k < c, 0, 1)
@@ -161,16 +163,37 @@
         pl.when(jnp.logical_and(c + onward >= 0, c + onward < n))(lambda: onward_copy(k, s, onward).start())
         pl.when(k != r)(lambda: left_copy(k, s).start())
 
-    for step in range(1, n):
-        for s in chunks:
+    for s in chunks:
+        for step in range(1, n):
             pl.when(c >= step)(lambda: arrived(c - step, s, 1))
             pl.when(c + step < n)(lambda: arrived(c + step, s, -1))
+            if step == 1 and s + ahead < len(chunks):
+                inner = jnp.logical_and(c > 0, c < n - 1)
+                pl.when(inner)(lambda: up(s + ahead).start())
+                pl.when(inner)(lambda: down(s + ahead).start())
 
     @pl.when(off)
     def _():
         @pl.loop(0, len(chunks))
         def _(s):
             multiply(chain, right, r, s)
+
+    for k in range(n):
+        pl.when(k != c)(lambda k=k: landed(gq0.at[k], gq_recv.at[k]))
+        pl.when(jnp.logical_or(k != c, off))(lambda k=k: landed(gp0.at[k], gp_recv.at[k]))
+
+    def start_gains(ref):
+        return [jnp.concatenate([ref[k, part : part + 1, :] for k in range(n)], axis=1) for part in range(2)]
+
+    gp = start_gains(gp0)
+    gq = start_gains(gq0)
+    lanes = 128
+
+    def lay_out(gains_row):
+        qr[...] = jnp.broadcast_to(gains_row[0], (lanes, block)).T
+        qi[...] = jnp.broadcast_to(gains_row[1], (lanes, block)).T
+
+    lay_out(gq)
 
     for step in range(1, n):
         landed(right.at[lax.rem(r + step, n)], right_recv.at[lax.rem(r + step, n)])
@@ -203,50 +226,46 @@
         vr[rows, :] = a * mr + b * mi
         vi[rows, :] = a * mi - b * mr
 
-    for k in range(n):
-        pl.when(k != c)(lambda k=k: landed(gq0.at[k], gq_recv.at[k]))
-        pl.when(jnp.logical_or(k != c, off))(lambda k=k: landed(gp0.at[k], gp_recv.at[k]))
-
-    def start_gains(ref):
-        return [jnp.concatenate([ref[k, part : part + 1, :] for k in range(n)], axis=1) for part in range(2)]
-
-    gp = start_gains(gp0)
-    gq = start_gains(gq0)
-    lanes = 128
-    tiles = block // lanes
-
     for it in range(ITERS):
-        gpr = jnp.broadcast_to(gp[0], (8, block))
-        gpi = jnp.broadcast_to(gp[1], (8, block))
-        qr[...] = jnp.broadcast_to(gq[0], (lanes, block)).T
-        qi[...] = jnp.broadcast_to(gq[1], (lanes, block)).T
-
-        def fold(x):
-            total = x[:, :lanes]
-            for t in range(1, tiles):
-                total = total + x[:, t * lanes : (t + 1) * lanes]
-            return total
-
-        def sums(s, carry):
-            sum_r, sum_i, sum_e = carry
-            rows = pl.ds(pl.multiple_of(s * 8, 8), 8)
-            wr, wi = vr[rows, :], vi[rows, :]
-            ar, ai = qr[rows, :], qi[rows, :]
-            norm = ar * ar + ai * ai
-            wide = lambda x: jnp.concatenate([x] * tiles, axis=1)
-            ar, ai, norm = wide(ar), wide(ai), wide(norm)
-            tr[rows, :] = fold(wr * gpr + wi * gpi)
-            ti[rows, :] = fold(wr * gpi - wi * gpr)
-            return (
-                sum_r + (wr * ar - wi * ai),
-                sum_i + (wr * ai + wi * ar),
-                sum_e + power[rows, :] * norm,
-            )
-
-        zero = jnp.zeros((8, block), jnp.float32)
-        sum_r, sum_i, sum_e = lax.fori_loop(0, block // 8, sums, (zero, zero, zero))
-        for part, value in enumerate((sum_r, sum_i, sum_e)):
-            abuf[it, part : part + 1, :] = jnp.sum(value, axis=0, keepdims=True)
+        if it > 0:
+            lay_out(gq)
+        width = max(block // 2, lanes)
+        for start in range(0, block, width):
+            columns = pl.ds(start, width)
+            gpr = jnp.broadcast_to(gp[0][:, start : start + width], (8, width))
+            gpi = jnp.broadcast_to(gp[1][:, start : start + width], (8, width))
+
+            def fold(x):
+                total = x[:, :lanes]
+                for t in range(lanes, width, lanes):
+                    total = total + x[:, t : t + lanes]
+                return total
+
+            def sums(s, carry):
+                sum_r, sum_i, sum_e = carry
+                rows = pl.ds(pl.multiple_of(s * 8, 8), 8)
+                wr, wi = vr[rows, columns], vi[rows, columns]
+                ar, ai = qr[rows, :], qi[rows, :]
+                norm = ar * ar + ai * ai
+                wide = lambda x: jnp.concatenate([x] * (width // lanes), axis=1)
+                ar, ai, norm = wide(ar), wide(ai), wide(norm)
+                row_r = fold(wr * gpr + wi * gpi)
+                row_i = fold(wr * gpi - wi * gpr)
+                if start > 0:
+                    row_r = row_r + tr[rows, :]
+                    row_i = row_i + ti[rows, :]
+                tr[rows, :] = row_r
+                ti[rows, :] = row_i
+                return (
+                    sum_r + (wr * ar - wi * ai),
+                    sum_i + (wr * ai + wi * ar),
+                    sum_e + power[rows, columns] * norm,
+                )
+
+            zero = jnp.zeros((8, width), jnp.float32)
+            found = lax.fori_loop(0, block // 8, sums, (zero, zero, zero), unroll=4)
+            for part, value in enumerate(found):
+                abuf[it, part : part + 1, columns] = jnp.sum(value, axis=0, keepdims=True)
         for part, ref in enumerate((tr, ti)):
             bbuf[it, part : part + 1, :] = jnp.sum(ref[...].T, axis=0, keepdims=True)
 

time: 155 us -> 151 us (0.974)
  Pallas kernels: 151 us -> 146 us
    pallas_call x1, Pallas kernels: 151 us -> 146 us  [square_body(): pl.pallas_call(functools.partial(calibrate, n), out_shape=jax.ShapeDtypeS...]
where the time goes in v4:
time: 151 us
  Pallas kernels  146 us (97%)
  local copies, waits for them, and re-layouts  4.54 us (3%)
    pallas_call x1, Pallas kernels, square_body(): pl.pallas_call(functools.partial(calibrate, n), out_shape=jax.ShapeDtypeS...  146 us
    unnamed x2, local copies, waits for them, and re-layouts  4.54 us

profile of v4, /device:TPU:0, one launch (start us, length us, event | category | flops | bytes accessed | tf_op | source)
XLA Modules:
  0.0 150.6 jit_solution(10365651098088845326)
XLA Ops:
  0.0 3.3 %copy.6 = bf16[1024,2,512]{2,0,1:T(8,128)(2,1)} copy(bf16[1024,2,512]{2,1,0:T(2,128)(2,1)} %param.3) | data formatting | bytes 4194304 | tf_op args[0]
  3.3 146.1 %shard_map.37 = f32[2,256]{1,0:T(2,128)} custom-call(bf16[2,1024,512]{2,1,0:T(8,128)(2,1)} %bitcast.3, bf16[1024,2,1024]{2,1,0:T(2,128)(2,1)} %sky.1, f32[2,256]{1,0:T(2,128)} %gains.1), custom_call_target="tpu_custom_call" | custom-call | flops 8589934592 | bytes 8388608 | tf_op jit(solution)/shard_map/pallas_call | solution.py:369
  149.3 1.3 copy.8

commit v5 on v4

--- a/solution.py
+++ b/solution.py
@@ -29,7 +29,7 @@
 
 
 def calibrate(
-    n, own, sky, gains, out, chain, left, right, vr, vi, power, model, qr, qi, tr, ti, gp0, gq0,
+    n, own, sky_model, gains, out, sky, chain, left, right, vr, vi, power, model, qr, qi, tr, ti, gp0, gq0,
     abuf, bbuf, ain, bin_, gin,
     up_send, fwd_send, chain_recv, left_send, left_recv, right_send, right_recv, local_sem,
     gp_send, gp_recv, gq_send, gq_recv, a_send, a_recv, b_send, b_recv, g_send, g_recv,
@@ -55,6 +55,9 @@
     diag = r == c
     off = r != c
 
+    sky_copy = pltpu.make_async_copy(sky_model, sky, local_sem.at[0])
+    sky_copy.start()
+
     barrier = pltpu.get_barrier_semaphore()
     for step in range(1, n * n):
         other = lax.rem(r * n + c + step, n * n)
@@ -108,6 +111,8 @@
     @pl.when(diag)
     def _():
         gp0[c] = gains[...]
+
+    sky_copy.wait()
 
     rows_step = 32
     lane = lax.broadcasted_iota(jnp.int32, (rows_step, block), 1) + c * block
@@ -139,8 +144,14 @@
             lax.dot_general, dimension_numbers=CONTRACT_LAST, preferred_element_type=jnp.float32
         )
         both = lambda x, y: jnp.concatenate([x, y], axis=1)
-        vr[rows, :] += dot(both(ar, ai), both(br, bi))
-        vi[rows, :] += dot(both(ai, -ar), both(br, bi))
+        found = dot(jnp.concatenate([both(ar, ai), both(ai, -ar)], axis=0), both(br, bi))
+        vr[rows, :] += found[:tile]
+        vi[rows, :] += found[tile:]
+
+    def square(ref, k):
+        @pl.loop(0, len(chunks))
+        def _(s):
+            multiply(ref, ref, k, s)
 
     @pl.when(diag)
     def _():
@@ -148,10 +159,8 @@
         copy.start()
         copy.wait()
 
-        @pl.loop(0, len(chunks))
-        def _(s):
-            multiply(left, left, r, s)
-            multiply(right, right, r, s)
+        square(left, r)
+        square(right, r)
 
     def onward_copy(k, s, onward):
         return remote(
@@ -195,28 +204,35 @@
 
     lay_out(gq)
 
-    for step in range(1, n):
-        landed(right.at[lax.rem(r + step, n)], right_recv.at[lax.rem(r + step, n)])
-
-    @pl.loop(0, len(chunks))
-    def _(s):
-        @pl.loop(1, n)
-        def _(step):
+    @pl.when(off)
+    def _():
+        for step in range(1, n):
             k = lax.rem(r + step, n)
-            rows = pl.ds(pl.multiple_of(s * tile, tile), tile)
-            landed(left.at[k, :, rows, :], left_recv.at[k, s])
-            pl.when(off)(lambda: multiply(left, right, k, s))
+            landed(right.at[k], right_recv.at[k])
+
+        @pl.loop(0, len(chunks))
+        def _(s):
+            @pl.loop(1, n)
+            def _(step):
+                k = lax.rem(r + step, n)
+                rows = pl.ds(pl.multiple_of(s * tile, tile), tile)
+                landed(left.at[k, :, rows, :], left_recv.at[k, s])
+                multiply(left, right, k, s)
 
     @pl.when(diag)
     def _():
         @pl.loop(1, n)
         def _(step):
             k = lax.rem(r + step, n)
-
-            @pl.loop(0, len(chunks))
-            def _(s):
-                multiply(left, left, k, s)
-                multiply(right, right, k, s)
+            landed(right.at[k], right_recv.at[k])
+            square(right, k)
+
+        @pl.loop(1, n)
+        def _(step):
+            k = lax.rem(r + step, n)
+            for s in chunks:
+                landed(part_of(left, k, s), left_recv.at[k, s])
+            square(left, k)
 
     @pl.loop(0, block // rows_step)
     def _(s):
@@ -369,9 +385,14 @@
     return pl.pallas_call(
         functools.partial(calibrate, n),
         out_shape=jax.ShapeDtypeStruct((2, share), f32),
-        in_specs=[pl.BlockSpec(memory_space=pltpu.VMEM)] * 3,
+        in_specs=[
+            pl.BlockSpec(memory_space=pltpu.VMEM),
+            pl.BlockSpec(memory_space=pl.ANY),
+            pl.BlockSpec(memory_space=pltpu.VMEM),
+        ],
         out_specs=pl.BlockSpec(memory_space=pltpu.VMEM),
         scratch_shapes=[
+            vmem(sky_model.shape, bf16),
             vmem(piece, bf16),
             vmem(piece, bf16),
             vmem(piece, bf16),

time: 151 us -> 141 us (0.934)
  Pallas kernels: 146 us -> 136 us
    pallas_call x1, Pallas kernels: 146 us -> 136 us  [square_body(): pl.pallas_call(functools.partial(calibrate, n), out_shape=jax.ShapeDtypeS...]
where the time goes in v5:
time: 141 us
  Pallas kernels  136 us (96%)
  local copies, waits for them, and re-layouts  4.54 us (3%)
    pallas_call x1, Pallas kernels, square_body(): pl.pallas_call(functools.partial(calibrate, n), out_shape=jax.ShapeDtypeS...  136 us
    unnamed x2, local copies, waits for them, and re-layouts  4.54 us

profile of v5, /device:TPU:0, one launch (start us, length us, event | category | flops | bytes accessed | tf_op | source)
XLA Modules:
  0.0 140.7 jit_solution(2892258451433779700)
XLA Ops:
  0.0 3.3 %copy.6 = bf16[1024,2,512]{2,0,1:T(8,128)(2,1)} copy(bf16[1024,2,512]{2,1,0:T(2,128)(2,1)} %param.3) | data formatting | bytes 4194304 | tf_op args[0]
  3.3 136.2 %shard_map.37 = f32[2,256]{1,0:T(2,128)} custom-call(bf16[2,1024,512]{2,1,0:T(8,128)(2,1)} %bitcast.3, bf16[1024,2,1024]{2,1,0:T(2,128)(2,1)} %sky_model.1, f32[2,256]{1,0:T(2,128)} %gains.1), custom_call_target="tpu_custom_call" | custom-call | flops 8589934592 | bytes 8388608 | tf_op jit(solution)/shard_map/pallas_call | solution.py:385
  139.5 1.3 copy.8

commit v6 on v5

--- a/solution.py
+++ b/solution.py
@@ -29,7 +29,7 @@
 
 
 def calibrate(
-    n, own, sky_model, gains, out, sky, chain, left, right, vr, vi, power, model, qr, qi, tr, ti, gp0, gq0,
+    n, samples, sky_model, gains, out, own, sky, chain, left, right, vr, vi, power, model, qr, qi, tr, ti, gp0, gq0,
     abuf, bbuf, ain, bin_, gin,
     up_send, fwd_send, chain_recv, left_send, left_recv, right_send, right_recv, local_sem,
     gp_send, gp_recv, gq_send, gq_recv, a_send, a_recv, b_send, b_recv, g_send, g_recv,
@@ -64,6 +64,14 @@
         pl.semaphore_signal(
             barrier, inc=1, device_id={"row": other // n, "col": lax.rem(other, n)}, device_id_type=MESH
         )
+
+    @pl.loop(0, block // 32)
+    def _(s):
+        rows = pl.ds(pl.multiple_of(s * 32, 32), 32)
+        pair = samples[rows].astype(jnp.float32)
+        own[0, rows, :] = pair[:, 0, :].astype(own.dtype)
+        own[1, rows, :] = pair[:, 1, :].astype(own.dtype)
+
     pl.semaphore_wait(barrier, n * n - 1)
 
     def up(s):
@@ -376,7 +384,6 @@
 def square_body(n, samples, sky_model, initial_gains):
     block, _, times = samples.shape
     half = times // 2
-    parts = samples.transpose(1, 0, 2)
     share = initial_gains.shape[1]
     dma = pltpu.SemaphoreType.DMA
     vmem = pltpu.VMEM
@@ -392,6 +399,7 @@
         ],
         out_specs=pl.BlockSpec(memory_space=pltpu.VMEM),
         scratch_shapes=[
+            vmem((2, block, times), bf16),
             vmem(sky_model.shape, bf16),
             vmem(piece, bf16),
             vmem(piece, bf16),
@@ -423,7 +431,7 @@
         cost_estimate=pl.CostEstimate(
             flops=8 * block * block * times * n // 2, bytes_accessed=8 * block * block, transcendentals=0
         ),
-    )(parts, sky_model, initial_gains)
+    )(samples, sky_model, initial_gains)
 
 
 def body(samples, sky_model, initial_gains):

time: 141 us -> 140 us (level)
  local copies, waits for them, and re-layouts: 4.54 us -> 1.26 us
  Pallas kernels: 136 us -> 138 us
    unnamed x2 -> x1, local copies, waits for them, and re-layouts: 4.54 us -> 1.26 us
    pallas_call x1, Pallas kernels: 136 us -> 138 us  [square_body(): pl.pallas_call(functools.partial(calibrate, n), out_shape=jax.ShapeDtypeS...]
where the time goes in v6:
time: 140 us
  Pallas kernels  138 us (99%)
    pallas_call x1, Pallas kernels, square_body(): pl.pallas_call(functools.partial(calibrate, n), out_shape=jax.ShapeDtypeS...  138 us

profile of v6, /device:TPU:0, one launch (start us, length us, event | category | flops | bytes accessed | tf_op | source)
XLA Modules:
  0.0 139.6 jit_solution(15938406139835183492)
XLA Ops:
  0.0 138.4 %shard_map.37 = f32[2,256]{1,0:T(2,128)} custom-call(bf16[1024,2,512]{2,1,0:T(2,128)(2,1)} %samples.1, bf16[1024,2,1024]{2,1,0:T(2,128)(2,1)} %sky_model.1, f32[2,256]{1,0:T(2,128)} %gains.1), custom_call_target="tpu_custom_call" | custom-call | flops 8589934592 | bytes 8388608 | tf_op jit(solution)/shard_map/pallas_call | solution.py:392
  138.4 1.3 copy.5
